TPU v7x, 256 devices: a whole 4x4x8 slice. The times are simulated.
256 devices in a mesh: section: 8 (over z_hi, core), expert: 32 (over z_lo, x, y).
Axes of the slice: x: 4, y: 4, z: 8 (z_hi: 4, z_lo: 2; z = z_hi * 2 + z_lo), core: 2. Of those that a mesh axis runs over, the one named last changes fastest.
Arguments:
- tokens: bfloat16 [8, 8192, 2560], P('section', 'expert'), may hold values from -6 to 6
- routes: int32 [8, 8192, 6], P('section', 'expert'), may hold values from 0 to 159, all different within a row
- route_weights: float32 [8, 8192, 6], P('section', 'expert'), may hold values from 0.05 to 1
- cotangent: bfloat16 [8, 8192, 2560], P('section', 'expert'), may hold values from -6 to 6
- w_gate: bfloat16 [8, 2560, 8192], P('section', None, 'expert'), as said below
- w_up: bfloat16 [8, 2560, 8192], P('section', None, 'expert'), as said below
- w_down: bfloat16 [8, 8192, 2560], P('section', 'expert'), as said below
Outputs:
- mixed: bfloat16 [8, 8192, 2560], P('section', 'expert')
- grad_tokens: bfloat16 [8, 8192, 2560], P('section', 'expert')
- grad_gate: bfloat16 [8, 2560, 8192], P('section', None, 'expert')
- grad_up: bfloat16 [8, 2560, 8192], P('section', None, 'expert')
- grad_down: bfloat16 [8, 8192, 2560], P('section', 'expert')
Inputs may be any that keep to these rules, and one draw needn't show every extreme that they name: w_gate[g] equals w_gate[7 - g] for every g. w_up[g] equals w_up[7 - g] for every g. w_down[g] equals w_down[7 - g] for every g.
All inputs are finite; a program needn't handle non-finite values.
Results may differ from a plain program's by a relative error of at most 0.0065.
Values may be sent and summed in bfloat16 or wider, within the bound.
A program may use at most 128 MiB of HBM per device.

v0:
```python
import jax
import jax.numpy as jnp
from jax import lax
from jax.sharding import PartitionSpec as P

SPLIT = 4
CAP = 16


def from_partner(x, axis, stride):
    return lax.ppermute(x, axis, [(i, i ^ 1 << stride) for i in range(lax.axis_size(axis))])


def inner(left, right):
    return lax.dot_general(
        left, right, (((0,), (0,)), ((), ())), preferred_element_type=jnp.float32
    )


def outer(left, right):
    return lax.dot_general(
        left, right, (((1,), (1,)), ((), ())), preferred_element_type=jnp.float32
    )


def per_device(tokens, routes, route_weights, cotangent, w_gate, w_up, w_down):
    local_x = tokens[0]
    local_ids = routes[0]
    local_cw = route_weights[0]
    local_dy = cotangent[0]
    gate_cols = w_gate[0]
    up_cols = w_up[0]
    down_rows = w_down[0]
    n_expert = lax.axis_size("expert")
    n_section = lax.axis_size("section")
    window = n_expert // SPLIT
    hid_dev = gate_cols.shape[1]
    width = local_x.shape[1]
    onehot = local_ids[:, :, None] == jnp.arange(window, dtype=jnp.int32)[None, None, :]
    hits = jnp.sum(onehot.astype(jnp.int32), axis=1)
    weight = jnp.sum(jnp.where(onehot, local_cw[:, :, None], jnp.zeros((), local_cw.dtype)), axis=1)
    slot = jnp.cumsum(hits, axis=0) - hits
    kept = (hits > 0) & (slot < CAP)
    places = jnp.arange(CAP, dtype=jnp.int32)[None, :, None]
    select = kept.T[:, None, :] & (slot.T[:, None, :] == places)
    select_bf = select.astype(jnp.bfloat16)
    select_f32 = select.astype(jnp.float32)
    rows = jnp.einsum("ect,td->ecd", select_bf, local_x, preferred_element_type=jnp.float32).astype(
        jnp.bfloat16
    )
    scale = jnp.einsum("ect,te->ec", select_f32, weight, precision=lax.Precision.HIGHEST)
    picked_dy = jnp.einsum("ect,td->ecd", select_bf, local_dy, preferred_element_type=jnp.float32)
    grad_rows = (scale[:, :, None] * picked_dy).astype(jnp.bfloat16)

    def spread(values):
        wide = jnp.broadcast_to(values[:, None], (window, SPLIT, CAP, width))
        return wide.reshape(n_expert, CAP, width)

    def combine(returned):
        return jnp.sum(returned.astype(jnp.float32).reshape(window, SPLIT, CAP, width), axis=1)

    recv_x = lax.all_to_all(spread(rows), "expert", split_axis=0, concat_axis=0, tiled=True)
    flat_x = recv_x.reshape(n_expert * CAP, width)
    gate = jnp.dot(flat_x, gate_cols, preferred_element_type=jnp.float32)
    up = jnp.dot(flat_x, up_cols, preferred_element_type=jnp.float32)
    sig = jax.nn.sigmoid(gate)
    hidden = (gate * sig * up).astype(jnp.bfloat16)
    partial_out = jnp.dot(hidden, down_rows, preferred_element_type=jnp.float32).astype(
        jnp.bfloat16
    )
    partial_out = partial_out.reshape(n_expert, CAP, width)
    returned = lax.all_to_all(partial_out, "expert", split_axis=0, concat_axis=0, tiled=True)
    recv_g = lax.all_to_all(spread(grad_rows), "expert", split_axis=0, concat_axis=0, tiled=True)
    flat_g = recv_g.reshape(n_expert * CAP, width)
    dh = outer(flat_g, down_rows)
    dgate = (dh * up * sig * (1.0 + gate * (1.0 - sig))).astype(jnp.bfloat16)
    dup = (dh * gate * sig).astype(jnp.bfloat16)
    grad_gate_own = inner(flat_x, dgate).astype(jnp.bfloat16)
    grad_up_own = inner(flat_x, dup).astype(jnp.bfloat16)
    grad_down_own = inner(hidden, flat_g).astype(jnp.bfloat16)
    back = (
        (outer(dgate, gate_cols) + outer(dup, up_cols))
        .astype(jnp.bfloat16)
        .reshape(n_expert, CAP, width)
    )
    back_returned = lax.all_to_all(back, "expert", split_axis=0, concat_axis=0, tiled=True)
    expert_out = combine(returned)
    mixed = jnp.einsum(
        "ect,ecd->td", select_f32, scale[:, :, None] * expert_out, precision=lax.Precision.HIGHEST
    ).astype(jnp.bfloat16)
    back_sum = combine(back_returned)
    grad_in = jnp.einsum(
        "ect,ecd->td", select_f32, back_sum, precision=lax.Precision.HIGHEST
    ).astype(jnp.bfloat16)
    flat_own = jnp.concatenate(
        [grad_gate_own.reshape(-1), grad_up_own.reshape(-1), grad_down_own.reshape(-1)]
    )
    partner = flat_own
    for bit in range(n_section.bit_length() - 1):
        partner = from_partner(partner, "section", bit)
    total = (flat_own.astype(jnp.float32) + partner.astype(jnp.float32)).astype(jnp.bfloat16)
    block = width * hid_dev
    grad_gate = total[:block].reshape(width, hid_dev)
    grad_up = total[block : 2 * block].reshape(width, hid_dev)
    grad_down = total[2 * block :].reshape(hid_dev, width)
    return (mixed[None], grad_in[None], grad_gate[None], grad_up[None], grad_down[None])


def solution(mesh):
    return jax.shard_map(
        per_device,
        mesh=mesh,
        in_specs=(
            P("section", "expert", None),
            P("section", "expert", None),
            P("section", "expert", None),
            P("section", "expert", None),
            P("section", None, "expert"),
            P("section", None, "expert"),
            P("section", "expert", None),
        ),
        out_specs=(
            P("section", "expert", None),
            P("section", "expert", None),
            P("section", None, "expert"),
            P("section", None, "expert"),
            P("section", "expert", None),
        ),
        check_vma=False,
    )
```

profile of v0, /device:TPU:4, one launch (start us, length us, event | category | flops | bytes accessed | tf_op | source)
XLA Modules:
  0.0 485.4 jit_solution(7873819085642212021)
XLA Ops:
  5.9 9.1 %all-to-all-start = ((bf16[32,16,2560]{2,1,0:T(8,128)(2,1)}), bf16[32,16,2560]{2,1,0:T(8,128)(2,1)}, u32[]{:S(2)}, u32[]{:S(2)}) async-start(bf16[32,16,2560]{2,1,0:T(8,128)(2,1)} %bitcast.94), calls=%async_computation | async-start | bytes 5242880 | tf_op jit(solution)/shard_map/all_to_all | solution.py:62
  15.6 32.5 %all-to-all-done = bf16[32,16,2560]{2,1,0:T(8,128)(2,1)} async-done(((bf16[32,16,2560]{2,1,0:T(8,128)(2,1)}), bf16[32,16,2560]{2,1,0:T(8,128)(2,1)}, u32[]{:S(2)}, u32[]{:S(2)}) %all-to-all-start) | async-done | bytes 2621472 | tf_op jit(solution)/shard_map/all_to_all | solution.py:62
  49.9 7.6 %all-to-all-start.2 = ((bf16[32,16,2560]{2,1,0:T(8,128)(2,1)}), bf16[32,16,2560]{2,1,0:T(8,128)(2,1)}, u32[]{:S(2)}, u32[]{:S(2)}) async-start(bf16[32,16,2560]{2,1,0:T(8,128)(2,1)} %bitcast.95), calls=%async_computation.2 | async-start | bytes 5242880 | tf_op jit(solution)/shard_map/all_to_all | solution.py:73
  57.5 3.5 fusion.12
  61.0 2.6 fusion.16
  63.7 26.8 %all-to-all-done.2 = bf16[32,16,2560]{2,1,0:T(8,128)(2,1)} async-done(((bf16[32,16,2560]{2,1,0:T(8,128)(2,1)}), bf16[32,16,2560]{2,1,0:T(8,128)(2,1)}, u32[]{:S(2)}, u32[]{:S(2)}) %all-to-all-start.2) | async-done | bytes 2621472 | tf_op jit(solution)/shard_map/all_to_all | solution.py:73
  90.5 2.7 multiply_convert_fusion
  93.2 2.6 fusion.5
  98.4 2.6 fusion.6
  102.4 3.7 convolution_convert_fusion.1
  106.1 3.9 reshape.104
  114.4 2.4 add_convert_fusion.1
  116.8 8.1 %all-to-all-start.3 = ((bf16[32,16,2560]{2,1,0:T(8,128)(2,1)}), bf16[32,16,2560]{2,1,0:T(8,128)(2,1)}, u32[]{:S(2)}, u32[]{:S(2)}) async-start(bf16[32,16,2560]{2,1,0:T(8,128)(2,1)} %bitcast.93), calls=%async_computation.3 | async-start | bytes 5242880 | tf_op jit(solution)/shard_map/all_to_all | solution.py:86
  125.0 3.4 collective-permute-start.1
  130.6 54.3 %all-to-all-done.3 = bf16[32,16,2560]{2,1,0:T(8,128)(2,1)} async-done(((bf16[32,16,2560]{2,1,0:T(8,128)(2,1)}), bf16[32,16,2560]{2,1,0:T(8,128)(2,1)}, u32[]{:S(2)}, u32[]{:S(2)}) %all-to-all-start.3) | async-done | bytes 2621472 | tf_op jit(solution)/shard_map/all_to_all | solution.py:86
  185.0 6.3 %all-to-all-start.1 = ((bf16[32,16,2560]{2,1,0:T(8,128)(2,1)}), bf16[32,16,2560]{2,1,0:T(8,128)(2,1)}, u32[]{:S(2)}, u32[]{:S(2)}) async-start(bf16[32,16,2560]{2,1,0:T(8,128)(2,1)} %bitcast.92), calls=%async_computation.1 | async-start | bytes 5242880 | tf_op jit(solution)/shard_map/all_to_all | solution.py:72
  191.3 106.1 %collective-permute-done.1 = bf16[1966080]{0:T(1024)(128)(2,1)} collective-permute-done((bf16[1966080]{0:T(1024)(128)(2,1)}, bf16[1966080]{0:T(1024)(128)(2,1)}, u32[]{:S(2)}, u32[]{:S(2)}) %collective-permute-start.1) | collective-permute-done | bytes 3932192 | tf_op jit(solution)/shard_map/ppermute | solution.py:11
  297.4 5.7 %collective-permute-start.2 = (bf16[1966080]{0:T(1024)(128)(2,1)}, bf16[1966080]{0:T(1024)(128)(2,1)}, u32[]{:S(2)}, u32[]{:S(2)}) collective-permute-start(bf16[1966080]{0:T(1024)(128)(2,1)} %collective-permute-done.1), channel_id=1, source_target_pairs={{0,128},{32,160},{64,192},{96,224},{128,0},{160,32},{192,64},{224,... | collective-permute-start | bytes 11796488 | tf_op jit(solution)/shard_map/ppermute | solution.py:11
  305.4 2.3 convert_reduce_fusion.1
  310.1 2.4 fusion.3
  312.5 159.9 %collective-permute-done.2 = bf16[1966080]{0:T(1024)(128)(2,1)} collective-permute-done((bf16[1966080]{0:T(1024)(128)(2,1)}, bf16[1966080]{0:T(1024)(128)(2,1)}, u32[]{:S(2)}, u32[]{:S(2)}) %collective-permute-start.2) | collective-permute-done | bytes 3932192 | tf_op jit(solution)/shard_map/ppermute | solution.py:11
  472.4 2.6 add_convert_fusion
  476.7 3.2 slice.48
  479.9 3.2 slice.50
  (48 shorter events, 26.9 us)
Async XLA Ops:
  0.6 89.8 %copy-start = (bf16[1,256,2560]{2,1,0:T(8,128)(2,1)S(1)}, bf16[1,256,2560]{2,1,0:T(8,128)(2,1)}, u32[]{:S(2)}) copy-start(bf16[1,256,2560]{2,1,0:T(8,128)(2,1)} %param.13) | copy-start | bytes 3932164
  5.9 9.1 %copy-start.8 = (f32[1,256,6]{1,0,2:T(1,128)S(1)}, f32[1,256,6]{1,0,2:T(1,128)}, u32[]{:S(2)}) copy-start(f32[1,256,6]{1,0,2:T(1,128)} %param.9) | copy-start | bytes 18436
  5.9 9.4 %copy-start.7 = (bf16[1,256,2560]{2,1,0:T(8,128)(2,1)S(1)}, bf16[1,256,2560]{2,1,0:T(8,128)(2,1)}, u32[]{:S(2)}) copy-start(bf16[1,256,2560]{2,1,0:T(8,128)(2,1)} %param.10) | copy-start | bytes 3932164
  5.9 42.2 %all-to-all-start = ((bf16[32,16,2560]{2,1,0:T(8,128)(2,1)}), bf16[32,16,2560]{2,1,0:T(8,128)(2,1)}, u32[]{:S(2)}, u32[]{:S(2)}) async-start(bf16[32,16,2560]{2,1,0:T(8,128)(2,1)} %bitcast.94), calls=%async_computation | async-start | bytes 5242880 | tf_op jit(solution)/shard_map/all_to_all | solution.py:62
  49.9 7.6 %copy-start.5 = (bf16[1,2560,256]{2,1,0:T(8,128)(2,1)S(1)}, bf16[1,2560,256]{2,1,0:T(8,128)(2,1)}, u32[]{:S(2)}) copy-start(bf16[1,2560,256]{2,1,0:T(8,128)(2,1)} %param.12) | copy-start | bytes 3932164
  49.9 40.6 %all-to-all-start.2 = ((bf16[32,16,2560]{2,1,0:T(8,128)(2,1)}), bf16[32,16,2560]{2,1,0:T(8,128)(2,1)}, u32[]{:S(2)}, u32[]{:S(2)}) async-start(bf16[32,16,2560]{2,1,0:T(8,128)(2,1)} %bitcast.95), calls=%async_computation.2 | async-start | bytes 5242880 | tf_op jit(solution)/shard_map/all_to_all | solution.py:73
  57.5 3.5 copy-start.3
  61.0 29.5 %copy-start.9 = (f32[512,256]{1,0:T(8,128)S(1)}, f32[512,256]{1,0:T(8,128)}, u32[]{:S(2)}) copy-start(f32[512,256]{1,0:T(8,128)} %fusion.12) | copy-start | bytes 1572868
  110.0 1.8 copy-start.2
  111.7 1.8 copy-start.4
  112.9 1.5 copy-start.6
  112.9 12.0 %collective-permute-start = (bf16[1966080]{0:T(1024)(128)(2,1)}, bf16[1966080]{0:T(1024)(128)(2,1)}, u32[]{:S(2)}, u32[]{:S(2)}) collective-permute-start(bf16[1966080]{0:T(1024)(128)(2,1)} %constant_dynamic-update-slice_fusion), channel_id=1, source_target_pairs={{0,32},{32,0},{64,96},{96,64},{128,160},{160,128},{192,224},{224,1... | collective-permute-start | bytes 11796488 | tf_op jit(solution)/shard_map/ppermute | solution.py:11
  116.8 68.2 %all-to-all-start.3 = ((bf16[32,16,2560]{2,1,0:T(8,128)(2,1)}), bf16[32,16,2560]{2,1,0:T(8,128)(2,1)}, u32[]{:S(2)}, u32[]{:S(2)}) async-start(bf16[32,16,2560]{2,1,0:T(8,128)(2,1)} %bitcast.93), calls=%async_computation.3 | async-start | bytes 5242880 | tf_op jit(solution)/shard_map/all_to_all | solution.py:86
  125.0 172.5 %collective-permute-start.1 = (bf16[1966080]{0:T(1024)(128)(2,1)}, bf16[1966080]{0:T(1024)(128)(2,1)}, u32[]{:S(2)}, u32[]{:S(2)}) collective-permute-start(bf16[1966080]{0:T(1024)(128)(2,1)} %collective-permute-done), channel_id=1, source_target_pairs={{0,64},{32,96},{64,0},{96,32},{128,192},{160,224},{192,128},{224,1... | collective-permute-start | bytes 11796488 | tf_op jit(solution)/shard_map/ppermute | solution.py:11
  185.0 120.4 %all-to-all-start.1 = ((bf16[32,16,2560]{2,1,0:T(8,128)(2,1)}), bf16[32,16,2560]{2,1,0:T(8,128)(2,1)}, u32[]{:S(2)}, u32[]{:S(2)}) async-start(bf16[32,16,2560]{2,1,0:T(8,128)(2,1)} %bitcast.92), calls=%async_computation.1 | async-start | bytes 5242880 | tf_op jit(solution)/shard_map/all_to_all | solution.py:72
  297.4 174.9 %collective-permute-start.2 = (bf16[1966080]{0:T(1024)(128)(2,1)}, bf16[1966080]{0:T(1024)(128)(2,1)}, u32[]{:S(2)}, u32[]{:S(2)}) collective-permute-start(bf16[1966080]{0:T(1024)(128)(2,1)} %collective-permute-done.1), channel_id=1, source_target_pairs={{0,128},{32,160},{64,192},{96,224},{128,0},{160,32},{192,64},{224,... | collective-permute-start | bytes 11796488 | tf_op jit(solution)/shard_map/ppermute | solution.py:11
  310.1 162.3 %copy-start.1 = (bf16[1966080]{0:T(1024)(128)(2,1)S(1)}, bf16[1966080]{0:T(1024)(128)(2,1)}, u32[]{:S(2)}) copy-start(bf16[1966080]{0:T(1024)(128)(2,1)} %constant_dynamic-update-slice_fusion) | copy-start | bytes 11796484
where the time goes:
time: 486 us; the launch traced here: 485 us
  waiting for transfers between devices  380 us (78%)
  starting transfers between devices  40.2 us (8%)
  matrix products  30.3 us (6%)
  local copies, waits for them, and re-layouts  26.4 us (5%)
  other arithmetic  7.95 us (2%)
    ppermute x3, waiting for transfers between devices, from_partner(): lax.ppermute(x, axis, [(i, i ^ 1 << stride) for i in range(lax.axis_size(...  266 us
    all_to_all x1, waiting for transfers between devices, per_device(): lax.all_to_all(back, 'expert', split_axis=0, concat_axis=0, tiled=True)  54.3 us
    all_to_all x1, waiting for transfers between devices, per_device(): lax.all_to_all(spread(rows), 'expert', split_axis=0, concat_axis=0, tiled...  32.5 us
    all_to_all x1, waiting for transfers between devices, per_device(): lax.all_to_all(spread(grad_rows), 'expert', split_axis=0, concat_axis=0,...  26.8 us
  transfers between devices with their start and end apart: 7, of which 5 were waited for; matrix products, arithmetic and copies ran while one was open for 4% of the time, Pallas kernels for 0%

commit v1 on v0

v1 whole, which is shorter than its diff:
```python
import functools

import jax
import jax.numpy as jnp
from jax import lax
from jax.experimental import pallas as pl
from jax.experimental.pallas import tpu as pltpu
from jax.sharding import PartitionSpec as P

SPLIT = 4
CAP = 16
MESH = pl.DeviceIdType.MESH
F32 = jnp.float32
BF16 = jnp.bfloat16

OWN, RIGHT, LEFT, OPPOSITE = range(4)


def nt(left, right):
    return lax.dot_general(left, right, (((1,), (1,)), ((), ())), preferred_element_type=F32)


def tn(left, right):
    return lax.dot_general(left, right, (((0,), (0,)), ((), ())), preferred_element_type=F32)


def nn(left, right):
    return jnp.dot(left, right, preferred_element_type=F32)


def kernel(
    n_section, window, step,
    tokens, routes, route_weights, cotangent, gate_hbm, up_hbm, down_hbm,
    mixed, grad_in, grad_gate, grad_up, grad_down,
    w_gate, w_up, w_down, send, held, weights_hi, weights_lo, chosen,
    gate_val, up_val, act, part, via, last, ret_send, ret,
    sum_gate, sum_up, sum_down,
    w_sem, a_send, a_recv, y_send, y_recv, r_send, r_recv, e_send, e_recv,
):
    group = lax.axis_index("section")
    index = lax.axis_index("expert")
    expert = index // SPLIT
    quarter = index % SPLIT
    mirror = n_section - 1 - group
    shard = window * CAP
    half = shard // 2
    n_tok, width = tokens.shape

    right = (group, expert * SPLIT + (quarter + 1) % SPLIT)
    left = (group, expert * SPLIT + (quarter + SPLIT - 1) % SPLIT)

    def at_expert(g, j):
        return (g, (expert + j) % window * SPLIT + quarter)

    weight_copies = [
        pltpu.make_async_copy(src, dst, w_sem.at[i])
        for i, (src, dst) in enumerate(((gate_hbm, w_gate), (up_hbm, w_up), (down_hbm, w_down)))
    ]
    for copy in weight_copies:
        copy.start()

    barrier = pltpu.get_barrier_semaphore()
    friends = [right, left]
    friends += [at_expert(group, j) for j in range(1, window)]
    friends += [at_expert(mirror, j) for j in range(window)]
    for friend in friends:
        pl.semaphore_signal(barrier, inc=1, device_id=friend, device_id_type=MESH)

    def remote(src, dst, send_sem, recv_sem, device):
        pltpu.make_async_remote_copy(
            src_ref=src, dst_ref=dst, send_sem=send_sem, recv_sem=recv_sem,
            device_id=device, device_id_type=MESH,
        ).start()

    def settle(ref, sem):
        pltpu.make_async_copy(ref, ref, sem).wait()

    def chunks(body, total=width):
        def run(i, carry):
            body(pl.ds(pl.multiple_of(i * step, step), step))
            return carry

        lax.fori_loop(0, total // step, run, 0)

    column = lax.broadcasted_iota(jnp.int32, (n_tok, shard), 1)
    wanted = (expert + column // CAP) % window
    hits = jnp.zeros((n_tok, shard), F32)
    weight = jnp.zeros((n_tok, shard), F32)
    for k in range(routes.shape[1]):
        same = routes[:, k : k + 1] == wanted
        hits = jnp.where(same, 1.0, hits)
        weight = weight + jnp.where(same, route_weights[:, k : k + 1], 0.0)
    before = lax.broadcasted_iota(jnp.int32, (n_tok, n_tok), 0) > lax.broadcasted_iota(
        jnp.int32, (n_tok, n_tok), 1
    )
    slot = nn(jnp.where(before, 1.0, 0.0).astype(BF16), hits.astype(BF16))
    kept = (hits > 0.0) & (slot == (column % CAP).astype(F32))
    select = jnp.where(kept, 1.0, 0.0)
    weight = jnp.where(kept, weight, 0.0)
    high = weight.astype(BF16)
    weights_hi[...] = high
    weights_lo[...] = (weight - high.astype(F32)).astype(BF16)
    chosen[...] = select.astype(BF16)
    select_t = jnp.transpose(select).astype(BF16)
    scale = jnp.sum(jnp.transpose(weight), axis=1, keepdims=True)

    def pick_rows(at):
        send[0, :, at] = nn(select_t, tokens[:, at]).astype(BF16)
        held[0, 0, :CAP, at] = send[0, :CAP, at]

    def pick_scaled(at):
        send[1, :, at] = (scale * nn(select_t, cotangent[:, at])).astype(BF16)
        held[1, 0, :CAP, at] = send[1, :CAP, at]

    def block(j):
        return pl.ds(j * CAP, CAP)

    def dispatch(t, k):
        g = (group, mirror)[k]
        for j in range(1 - k, window):
            remote(
                send.at[t, block(j)], held.at[t, k, block(j)],
                a_send.at[t, k], a_recv.at[t, k, j // (window // 2)], at_expert(g, j),
            )

    def rows_of(which, h=None):
        if h is None:
            return pl.ds(which * shard, shard)
        return pl.ds(which * shard + h * half, half)

    def gather(t, k):
        for h in range(2):
            skip = CAP if k == 0 and h == 0 else 0
            settle(held.at[t, k, pl.ds(h * half + skip, half - skip)], a_recv.at[t, k, h])
            mine = held.at[t, k, rows_of(OWN, h)]
            remote(mine, held.at[t, k, rows_of(LEFT, h)], y_send.at[t, k, h], y_recv.at[t, k, h], right)
            remote(mine, held.at[t, k, rows_of(RIGHT, h)], y_send.at[t, k, 2 + h], y_recv.at[t, k, 2 + h], left)

    def forward(t, k):
        from_left = [(held.at[t, k, rows_of(LEFT, h)], y_recv.at[t, k, h]) for h in range(2)]
        from_right = [(held.at[t, k, rows_of(RIGHT, h)], y_recv.at[t, k, 2 + h]) for h in range(2)]
        settle(*from_right[0])
        remote(from_right[0][0], held.at[t, k, rows_of(OPPOSITE, 0)], y_send.at[t, k, 4], y_recv.at[t, k, 4], left)
        settle(*from_left[0])
        settle(*from_left[1])
        remote(from_left[1][0], held.at[t, k, rows_of(OPPOSITE, 1)], y_send.at[t, k, 5], y_recv.at[t, k, 5], right)
        settle(*from_right[1])

    def far(t, k):
        for h in range(2):
            settle(held.at[t, k, rows_of(OPPOSITE, h)], y_recv.at[t, k, 4 + h])

    def forward_pass(k, first, count):
        rows = pl.ds(first * shard, count * shard)
        x = held[0, k, rows]
        gate_val[rows] = nn(x, w_gate[...])
        up_val[rows] = nn(x, w_up[...])

    def backward_pass(k, first, count):
        rows = pl.ds(first * shard, count * shard)
        dh = nt(held[1, k, rows], w_down[...])
        gate, up = gate_val[rows], up_val[rows]
        sig = jax.nn.sigmoid(gate)
        act[0, k, rows] = (gate * sig * up).astype(BF16)
        act[1, k, rows] = (dh * up * sig * (1.0 + gate * (1.0 - sig))).astype(BF16)
        act[2, k, rows] = (dh * gate * sig).astype(BF16)

    def parts(first, count):
        rows = pl.ds(first * shard, count * shard)

        def one(at):
            part[0, rows, at] = nn(act[0, 0, rows], w_down[:, at]).astype(BF16)
            part[1, rows, at] = (
                nt(act[1, 0, rows], w_gate[at, :]) + nt(act[2, 0, rows], w_up[at, :])
            ).astype(BF16)

        chunks(one)

    def gradients(k, first, count, start, stop):
        rows = pl.ds(first * shard, count * shard)

        def one(at):
            x, g = held[0, k, rows, at], held[1, k, rows, at]
            terms = (tn(x, act[1, k, rows]), tn(x, act[2, k, rows]), tn(act[0, k, rows], g))
            where = ((at, slice(None)), (at, slice(None)), (slice(None), at))
            for total, out, term, place in zip((sum_gate, sum_up, sum_down), (grad_gate, grad_up, grad_down), terms, where):
                if not start:
                    term = total[place] + term
                if stop:
                    out[place] = term.astype(BF16)
                else:
                    total[place] = term

        chunks(one)

    chunks(pick_rows)
    pl.semaphore_wait(barrier, len(friends))
    dispatch(0, 0)
    chunks(pick_scaled)
    dispatch(1, 0)
    dispatch(0, 1)
    dispatch(1, 1)

    gather(0, 0)
    for copy in weight_copies:
        copy.wait()
    forward_pass(0, OWN, 1)
    gather(1, 0)
    backward_pass(0, OWN, 1)
    parts(OWN, 1)
    forward(0, 0)
    forward_pass(0, RIGHT, 2)
    forward(1, 0)
    backward_pass(0, RIGHT, 2)
    parts(RIGHT, 2)

    for t in range(2):
        remote(part.at[t, rows_of(RIGHT, 1)], last.at[t, rows_of(0, 1)], r_send.at[t, 3], r_recv.at[t, 3], right)
        remote(part.at[t, rows_of(LEFT, 0)], last.at[t, rows_of(1, 0)], r_send.at[t, 4], r_recv.at[t, 4], left)
    far(0, 0)
    forward_pass(0, OPPOSITE, 1)
    far(1, 0)
    backward_pass(0, OPPOSITE, 1)
    parts(OPPOSITE, 1)
    for t in range(2):
        remote(part.at[t, rows_of(OPPOSITE, 0)], via.at[t, 0], r_send.at[t, 0], r_recv.at[t, 0], right)
        remote(part.at[t, rows_of(OPPOSITE, 1)], via.at[t, 1], r_send.at[t, 1], r_recv.at[t, 1], left)
    gather(0, 1)
    gradients(0, OWN, 4, True, False)

    for t in range(2):
        settle(via.at[t, 0], r_recv.at[t, 0])
        rows = rows_of(RIGHT, 0)
        part[t, rows] = (part[t, rows].astype(F32) + via[t, 0].astype(F32)).astype(BF16)
        remote(part.at[t, rows], last.at[t, rows_of(0, 0)], r_send.at[t, 2], r_recv.at[t, 2], right)
        settle(via.at[t, 1], r_recv.at[t, 1])
        rows = rows_of(LEFT, 1)
        part[t, rows] = (part[t, rows].astype(F32) + via[t, 1].astype(F32)).astype(BF16)
        remote(part.at[t, rows], last.at[t, rows_of(1, 1)], r_send.at[t, 5], r_recv.at[t, 5], left)

    forward(0, 1)
    gather(1, 1)
    forward_pass(1, OWN, 3)

    for t in range(2):
        for h in range(2):
            settle(last.at[t, rows_of(0, h)], r_recv.at[t, 2 + h])
            settle(last.at[t, rows_of(1, h)], r_recv.at[t, 4 + h])
            rows = rows_of(OWN, h)
            total = part[t, rows].astype(F32) + last[t, rows_of(0, h)].astype(F32) + last[t, rows_of(1, h)].astype(F32)
            ret_send[t, rows] = total.astype(BF16)
        ret[t, :CAP] = ret_send[t, :CAP]
        for j in range(1, window):
            remote(
                ret_send.at[t, block(j)], ret.at[t, block(j)],
                e_send.at[t], e_recv.at[t], at_expert(group, window - j),
            )

    forward(1, 1)
    backward_pass(1, OWN, 3)
    far(0, 1)
    forward_pass(1, OPPOSITE, 1)
    gradients(1, OWN, 3, False, False)

    rest = pl.ds(CAP, shard - CAP)
    settle(ret.at[0, rest], e_recv.at[0])

    def combine_out(at):
        mixed[:, at] = (nn(weights_hi[...], ret[0, :, at]) + nn(weights_lo[...], ret[0, :, at])).astype(BF16)

    chunks(combine_out)
    settle(ret.at[1, rest], e_recv.at[1])

    def combine_back(at):
        grad_in[:, at] = nn(chosen[...], ret[1, :, at]).astype(BF16)

    chunks(combine_back)

    far(1, 1)
    backward_pass(1, OPPOSITE, 1)
    gradients(1, OPPOSITE, 1, False, True)

    for t in range(2):
        for k in range(2):
            left_out = CAP if k == 0 else 0
            settle(send.at[t, pl.ds(left_out, shard - left_out)], a_send.at[t, k])
            for i in range(6):
                settle(held.at[t, k, rows_of(OWN, 0)], y_send.at[t, k, i])
        for i in range(6):
            settle(via.at[t, 0], r_send.at[t, i])
        settle(ret_send.at[t, rest], e_send.at[t])


def solution(mesh):
    n_section = mesh.shape["section"]
    window = mesh.shape["expert"] // SPLIT

    def per_device(tokens, routes, route_weights, cotangent, w_gate, w_up, w_down):
        _, n_tok, width = tokens.shape
        hidden = w_gate.shape[2]
        shard = window * CAP
        rows = SPLIT * shard
        step = 512 if width % 512 == 0 else 128
        vmem = pl.BlockSpec(memory_space=pltpu.VMEM)
        hbm = pl.BlockSpec(memory_space=pl.ANY)
        dma = pltpu.SemaphoreType.DMA
        flops = 2 * rows * width * hidden * 15
        outs = pl.pallas_call(
            functools.partial(kernel, n_section, window, step),
            out_shape=(
                jax.ShapeDtypeStruct((n_tok, width), BF16),
                jax.ShapeDtypeStruct((n_tok, width), BF16),
                jax.ShapeDtypeStruct((width, hidden), BF16),
                jax.ShapeDtypeStruct((width, hidden), BF16),
                jax.ShapeDtypeStruct((hidden, width), BF16),
            ),
            in_specs=[vmem] * 4 + [hbm] * 3,
            out_specs=(vmem,) * 5,
            scratch_shapes=[
                pltpu.VMEM((width, hidden), BF16),
                pltpu.VMEM((width, hidden), BF16),
                pltpu.VMEM((hidden, width), BF16),
                pltpu.VMEM((2, shard, width), BF16),
                pltpu.VMEM((2, 2, rows, width), BF16),
                pltpu.VMEM((n_tok, shard), BF16),
                pltpu.VMEM((n_tok, shard), BF16),
                pltpu.VMEM((n_tok, shard), BF16),
                pltpu.VMEM((rows, hidden), F32),
                pltpu.VMEM((rows, hidden), F32),
                pltpu.VMEM((3, 2, rows, hidden), BF16),
                pltpu.VMEM((2, rows, width), BF16),
                pltpu.VMEM((2, 2, shard // 2, width), BF16),
                pltpu.VMEM((2, 2 * shard, width), BF16),
                pltpu.VMEM((2, shard, width), BF16),
                pltpu.VMEM((2, shard, width), BF16),
                pltpu.VMEM((width, hidden), F32),
                pltpu.VMEM((width, hidden), F32),
                pltpu.VMEM((hidden, width), F32),
                dma((3,)),
                dma((2, 2)),
                dma((2, 2, 2)),
                dma((2, 2, 6)),
                dma((2, 2, 6)),
                dma((2, 6)),
                dma((2, 6)),
                dma((2,)),
                dma((2,)),
            ],
            compiler_params=pltpu.CompilerParams(
                collective_id=0, has_side_effects=True, vmem_limit_bytes=60 * 2**20
            ),
            cost_estimate=pl.CostEstimate(flops=flops, bytes_accessed=2 * 8 * n_tok * width, transcendentals=0),
        )(tokens[0], routes[0], route_weights[0], cotangent[0], w_gate[0], w_up[0], w_down[0])
        return tuple(out[None] for out in outs)

    return jax.shard_map(
        per_device,
        mesh=mesh,
        in_specs=(
            P("section", "expert", None),
            P("section", "expert", None),
            P("section", "expert", None),
            P("section", "expert", None),
            P("section", None, "expert"),
            P("section", None, "expert"),
            P("section", "expert", None),
        ),
        out_specs=(
            P("section", "expert", None),
            P("section", "expert", None),
            P("section", None, "expert"),
            P("section", None, "expert"),
            P("section", "expert", None),
        ),
        check_vma=False,
    )
```

time: 486 us -> 175 us (0.36)
  waiting for transfers between devices: 380 us -> 0 us
  Pallas kernels: 0 us -> 159 us
  starting transfers between devices: 40.2 us -> 0 us
  matrix products: 30.3 us -> 0 us
  local copies, waits for them, and re-layouts: 26.4 us -> 12 us
  other arithmetic: 7.95 us -> 0 us
    ppermute x3 -> x0, waiting for transfers between devices: 266 us -> none  [from_partner(): lax.ppermute(x, axis, [(i, i ^ 1 << stride) for i in range(lax.axis_size(...]
    pallas_call x0 -> x1, Pallas kernels: none -> 159 us  [per_device(): pl.pallas_call(functools.partial(kernel, n_section, window, step), out_sh...]
    all_to_all x4 -> x0, waiting for transfers between devices: 114 us -> none  [the longest x1 54.3 us: per_device(): lax.all_to_all(back, 'expert', split_axis=0, concat_axis=0, tiled=True)]
    all_to_all x4 -> x0, starting transfers between devices: 31.2 us -> none  [the longest x1 9.13 us: per_device(): lax.all_to_all(spread(rows), 'expert', split_axis=0, concat_axis=0, tiled...]
    dot_general x14 -> x0, matrix products: 30.3 us -> none  [the longest x3 8.93 us: inner(): lax.dot_general(left, right, (((0,), (0,)), ((), ())), preferred_element_...]
    slice x5 -> x0, local copies, waits for them, and re-layouts: 10.6 us -> none  [the longest x2 4.04 us: per_device(): grad_down = total[2 * block:].reshape(hid_dev, width)]
    ppermute x3 -> x0, starting transfers between devices: 9.03 us -> none  [from_partner(): lax.ppermute(x, axis, [(i, i ^ 1 << stride) for i in range(lax.axis_size(...]
    unnamed x26 -> x15, local copies, waits for them, and re-layouts: 7.18 us -> 12 us
  transfers between devices with their start and end apart: 7 -> 0, of which waited for: 5 -> 0; matrix products, arithmetic and copies ran while one was open for 4% -> 0% of each run, Pallas kernels for 0% -> 0%
where the time goes in v1:
time: 175 us; the launch traced here: 171 us
  Pallas kernels  159 us (91%)
  local copies, waits for them, and re-layouts  12 us (7%)
    pallas_call x1, Pallas kernels, per_device(): pl.pallas_call(functools.partial(kernel, n_section, window, step), out_sh...  159 us
    unnamed x15, local copies, waits for them, and re-layouts  12 us

profile of v1, /device:TPU:4, one launch (start us, length us, event | category | flops | bytes accessed | tf_op | source)
XLA Modules:
  0.0 171.5 jit_solution(7813905127241654621)
XLA Ops:
  0.6 1.5 copy.12
  2.1 1.5 copy.13
  3.6 158.9 %shard_map.110 = (bf16[256,2560]{1,0:T(8,128)(2,1)}, bf16[256,2560]{1,0:T(8,128)(2,1)}, bf16[2560,256]{1,0:T(8,128)(2,1)}, bf16[2560,256]{1,0:T(8,128)(2,1)}, bf16[256,2560]{1,0:T(8,128)(2,1)}) custom-call(bf16[256,2560]{1,0:T(8,128)(2,1)} %bitcast.19, s32[256,6]{1,0:T(8,128)} %bitcast.17, f32[256,6]{1,0:T(8,128)} %bitcast.18, bf16[256,2560]{1,0:T(8,128)(2,1)} %bitcast.20, ...), custom_call_target="tpu_custom_call" | custom-call | flops 10066329600 | bytes 10485760 | tf_op jit(solution)/shard_map/pallas_call | solution.py:308
  162.5 0.0 copy-start.3
  162.5 2.6 %copy.19 = bf16[1,256,2560]{2,1,0:T(8,128)(2,1)} copy(bf16[1,256,2560]{2,1,0:T(8,128)(2,1)} %bitcast.16) | data formatting | bytes 2621440
  165.0 0.0 copy-done.3
  165.0 0.0 copy-start.2
  165.0 1.1 copy.20
  166.1 0.7 copy-done.2
  166.8 0.0 copy-start.1
  166.8 1.1 copy.21
  167.9 0.7 copy-done.1
  168.6 0.0 copy-start
  168.6 1.1 copy.22
  169.7 0.7 copy-done
  170.4 1.1 copy.23
Async XLA Ops:
  162.5 2.6 %copy-start.3 = (bf16[256,2560]{1,0:T(8,128)(2,1)S(1)}, bf16[256,2560]{1,0:T(8,128)(2,1)}, u32[]{:S(2)}) copy-start(bf16[256,2560]{1,0:T(8,128)(2,1)} %get-tuple-element.11) | copy-start | bytes 3932164
  165.0 1.8 %copy-start.2 = (bf16[2560,256]{1,0:T(8,128)(2,1)S(1)}, bf16[2560,256]{1,0:T(8,128)(2,1)}, u32[]{:S(2)}) copy-start(bf16[2560,256]{1,0:T(8,128)(2,1)} %get-tuple-element.12) | copy-start | bytes 3932164
  166.8 1.8 %copy-start.1 = (bf16[2560,256]{1,0:T(8,128)(2,1)S(1)}, bf16[2560,256]{1,0:T(8,128)(2,1)}, u32[]{:S(2)}) copy-start(bf16[2560,256]{1,0:T(8,128)(2,1)} %get-tuple-element.13) | copy-start | bytes 3932164
  168.6 1.8 %copy-start = (bf16[256,2560]{1,0:T(8,128)(2,1)S(1)}, bf16[256,2560]{1,0:T(8,128)(2,1)}, u32[]{:S(2)}) copy-start(bf16[256,2560]{1,0:T(8,128)(2,1)} %get-tuple-element.14) | copy-start | bytes 3932164

commit v2 on v1

--- a/solution.py
+++ b/solution.py
@@ -14,6 +14,7 @@
 BF16 = jnp.bfloat16
 
 OWN, RIGHT, LEFT, OPPOSITE = range(4)
+ACROSS = ((0, 0), (0, 1))
 
 
 def nt(left, right):
@@ -30,12 +31,12 @@
 
 def kernel(
     n_section, window, step,
-    tokens, routes, route_weights, cotangent, gate_hbm, up_hbm, down_hbm,
-    mixed, grad_in, grad_gate, grad_up, grad_down,
-    w_gate, w_up, w_down, send, held, weights_hi, weights_lo, chosen,
+    tokens_hbm, routes, route_weights, cotangent_hbm, gate_hbm, up_hbm, down_hbm,
+    mixed_hbm, grad_in_hbm, grad_gate_hbm, grad_up_hbm, grad_down_hbm,
+    tokens, cotangent, w_gate, w_up, w_down, send, held, weights_hi, weights_lo, chosen,
     gate_val, up_val, act, part, via, last, ret_send, ret,
     sum_gate, sum_up, sum_down,
-    w_sem, a_send, a_recv, y_send, y_recv, r_send, r_recv, e_send, e_recv,
+    in_sem, out_sem, a_send, a_recv, y_send, y_recv, r_send, r_recv, e_send, e_recv,
 ):
     group = lax.axis_index("section")
     index = lax.axis_index("expert")
@@ -52,11 +53,12 @@
     def at_expert(g, j):
         return (g, (expert + j) % window * SPLIT + quarter)
 
-    weight_copies = [
-        pltpu.make_async_copy(src, dst, w_sem.at[i])
-        for i, (src, dst) in enumerate(((gate_hbm, w_gate), (up_hbm, w_up), (down_hbm, w_down)))
-    ]
-    for copy in weight_copies:
+    sources = (tokens_hbm, cotangent_hbm, gate_hbm, up_hbm, down_hbm)
+    places = (tokens, cotangent, w_gate, w_up, w_down)
+    loads = [pltpu.make_async_copy(src, dst, in_sem.at[i]) for i, (src, dst) in enumerate(zip(sources, places))]
+    results = (mixed_hbm, grad_in_hbm, grad_gate_hbm, grad_up_hbm, grad_down_hbm)
+    stores = [pltpu.make_async_copy(src, dst, out_sem.at[i]) for i, (src, dst) in enumerate(zip(places, results))]
+    for copy in loads[:2]:
         copy.start()
 
     barrier = pltpu.get_barrier_semaphore()
@@ -82,27 +84,23 @@
 
         lax.fori_loop(0, total // step, run, 0)
 
-    column = lax.broadcasted_iota(jnp.int32, (n_tok, shard), 1)
-    wanted = (expert + column // CAP) % window
-    hits = jnp.zeros((n_tok, shard), F32)
-    weight = jnp.zeros((n_tok, shard), F32)
-    for k in range(routes.shape[1]):
-        same = routes[:, k : k + 1] == wanted
+    row = lax.broadcasted_iota(jnp.int32, (shard, n_tok), 0)
+    wanted = (expert + row // CAP) % window
+    hits = jnp.zeros((shard, n_tok), F32)
+    weight = jnp.zeros((shard, n_tok), F32)
+    for k in range(routes.shape[0]):
+        same = routes[k : k + 1] == wanted
         hits = jnp.where(same, 1.0, hits)
-        weight = weight + jnp.where(same, route_weights[:, k : k + 1], 0.0)
-    before = lax.broadcasted_iota(jnp.int32, (n_tok, n_tok), 0) > lax.broadcasted_iota(
+        weight = weight + jnp.where(same, route_weights[k : k + 1], 0.0)
+    before = lax.broadcasted_iota(jnp.int32, (n_tok, n_tok), 0) < lax.broadcasted_iota(
         jnp.int32, (n_tok, n_tok), 1
     )
-    slot = nn(jnp.where(before, 1.0, 0.0).astype(BF16), hits.astype(BF16))
-    kept = (hits > 0.0) & (slot == (column % CAP).astype(F32))
+    slot = nn(hits.astype(BF16), jnp.where(before, 1.0, 0.0).astype(BF16))
+    kept = (hits > 0.0) & (slot == (row % CAP).astype(F32))
     select = jnp.where(kept, 1.0, 0.0)
     weight = jnp.where(kept, weight, 0.0)
-    high = weight.astype(BF16)
-    weights_hi[...] = high
-    weights_lo[...] = (weight - high.astype(F32)).astype(BF16)
-    chosen[...] = select.astype(BF16)
-    select_t = jnp.transpose(select).astype(BF16)
-    scale = jnp.sum(jnp.transpose(weight), axis=1, keepdims=True)
+    select_t = select.astype(BF16)
+    scale = jnp.sum(weight, axis=1, keepdims=True)
 
     def pick_rows(at):
         send[0, :, at] = nn(select_t, tokens[:, at]).astype(BF16)
@@ -128,27 +126,40 @@
             return pl.ds(which * shard, shard)
         return pl.ds(which * shard + h * half, half)
 
+    def both_ways(t, k, h, low, count):
+        def part_of(which):
+            return held.at[t, k, pl.ds(which * shard + h * half + low, count)]
+
+        remote(part_of(OWN), part_of(LEFT), y_send.at[t, k, h], y_recv.at[t, k, h], right)
+        remote(part_of(OWN), part_of(RIGHT), y_send.at[t, k, 2 + h], y_recv.at[t, k, 2 + h], left)
+
     def gather(t, k):
         for h in range(2):
             skip = CAP if k == 0 and h == 0 else 0
             settle(held.at[t, k, pl.ds(h * half + skip, half - skip)], a_recv.at[t, k, h])
-            mine = held.at[t, k, rows_of(OWN, h)]
-            remote(mine, held.at[t, k, rows_of(LEFT, h)], y_send.at[t, k, h], y_recv.at[t, k, h], right)
-            remote(mine, held.at[t, k, rows_of(RIGHT, h)], y_send.at[t, k, 2 + h], y_recv.at[t, k, 2 + h], left)
+            both_ways(t, k, h, skip, half - skip)
 
     def forward(t, k):
         from_left = [(held.at[t, k, rows_of(LEFT, h)], y_recv.at[t, k, h]) for h in range(2)]
         from_right = [(held.at[t, k, rows_of(RIGHT, h)], y_recv.at[t, k, 2 + h]) for h in range(2)]
         settle(*from_right[0])
-        remote(from_right[0][0], held.at[t, k, rows_of(OPPOSITE, 0)], y_send.at[t, k, 4], y_recv.at[t, k, 4], left)
+        if k == 0 or (t, 0) not in ACROSS:
+            remote(from_right[0][0], held.at[t, k, rows_of(OPPOSITE, 0)], y_send.at[t, k, 4], y_recv.at[t, k, 4], left)
         settle(*from_left[0])
         settle(*from_left[1])
-        remote(from_left[1][0], held.at[t, k, rows_of(OPPOSITE, 1)], y_send.at[t, k, 5], y_recv.at[t, k, 5], right)
+        if k == 0 or (t, 1) not in ACROSS:
+            remote(from_left[1][0], held.at[t, k, rows_of(OPPOSITE, 1)], y_send.at[t, k, 5], y_recv.at[t, k, 5], right)
         settle(*from_right[1])
 
     def far(t, k):
         for h in range(2):
-            settle(held.at[t, k, rows_of(OPPOSITE, h)], y_recv.at[t, k, 4 + h])
+            shard_half = held.at[t, k, rows_of(OPPOSITE, h)]
+            settle(shard_half, y_recv.at[t, k, 4 + h])
+            if k == 0 and (t, h) in ACROSS:
+                remote(
+                    shard_half, held.at[t, 1, rows_of(OPPOSITE, h)],
+                    y_send.at[t, 1, 4 + h], y_recv.at[t, 1, 4 + h], at_expert(mirror, 0),
+                )
 
     def forward_pass(k, first, count):
         rows = pl.ds(first * shard, count * shard)
@@ -183,7 +194,7 @@
             x, g = held[0, k, rows, at], held[1, k, rows, at]
             terms = (tn(x, act[1, k, rows]), tn(x, act[2, k, rows]), tn(act[0, k, rows], g))
             where = ((at, slice(None)), (at, slice(None)), (slice(None), at))
-            for total, out, term, place in zip((sum_gate, sum_up, sum_down), (grad_gate, grad_up, grad_down), terms, where):
+            for total, out, term, place in zip((sum_gate, sum_up, sum_down), places[2:], terms, where):
                 if not start:
                     term = total[place] + term
                 if stop:
@@ -193,31 +204,42 @@
 
         chunks(one)
 
+    loads[0].wait()
     chunks(pick_rows)
     pl.semaphore_wait(barrier, len(friends))
     dispatch(0, 0)
+    both_ways(0, 0, 0, 0, CAP)
+    loads[1].wait()
     chunks(pick_scaled)
     dispatch(1, 0)
+    both_ways(1, 0, 0, 0, CAP)
+    for copy in loads[2:]:
+        copy.start()
+    weight_t = jnp.transpose(weight)
+    high = weight_t.astype(BF16)
+    weights_hi[...] = high
+    weights_lo[...] = (weight_t - high.astype(F32)).astype(BF16)
+    chosen[...] = jnp.transpose(select).astype(BF16)
+
+    gather(0, 0)
     dispatch(0, 1)
+    gather(1, 0)
     dispatch(1, 1)
-
-    gather(0, 0)
-    for copy in weight_copies:
+    for copy in loads[2:]:
         copy.wait()
     forward_pass(0, OWN, 1)
-    gather(1, 0)
+    forward(0, 0)
     backward_pass(0, OWN, 1)
     parts(OWN, 1)
-    forward(0, 0)
     forward_pass(0, RIGHT, 2)
     forward(1, 0)
+    far(0, 0)
     backward_pass(0, RIGHT, 2)
     parts(RIGHT, 2)
 
     for t in range(2):
         remote(part.at[t, rows_of(RIGHT, 1)], last.at[t, rows_of(0, 1)], r_send.at[t, 3], r_recv.at[t, 3], right)
         remote(part.at[t, rows_of(LEFT, 0)], last.at[t, rows_of(1, 0)], r_send.at[t, 4], r_recv.at[t, 4], left)
-    far(0, 0)
     forward_pass(0, OPPOSITE, 1)
     far(1, 0)
     backward_pass(0, OPPOSITE, 1)
@@ -226,7 +248,7 @@
         remote(part.at[t, rows_of(OPPOSITE, 0)], via.at[t, 0], r_send.at[t, 0], r_recv.at[t, 0], right)
         remote(part.at[t, rows_of(OPPOSITE, 1)], via.at[t, 1], r_send.at[t, 1], r_recv.at[t, 1], left)
     gather(0, 1)
-    gradients(0, OWN, 4, True, False)
+    forward_pass(1, OWN, 1)
 
     for t in range(2):
         settle(via.at[t, 0], r_recv.at[t, 0])
@@ -238,9 +260,8 @@
         part[t, rows] = (part[t, rows].astype(F32) + via[t, 1].astype(F32)).astype(BF16)
         remote(part.at[t, rows], last.at[t, rows_of(1, 1)], r_send.at[t, 5], r_recv.at[t, 5], left)
 
-    forward(0, 1)
     gather(1, 1)
-    forward_pass(1, OWN, 3)
+    gradients(0, OWN, 4, True, False)
 
     for t in range(2):
         for h in range(2):
@@ -256,29 +277,37 @@
                 e_send.at[t], e_recv.at[t], at_expert(group, window - j),
             )
 
-    forward(1, 1)
-    backward_pass(1, OWN, 3)
+    backward_pass(1, OWN, 1)
+    gradients(1, OWN, 1, False, False)
+    forward(0, 1)
+    forward_pass(1, RIGHT, 2)
     far(0, 1)
     forward_pass(1, OPPOSITE, 1)
-    gradients(1, OWN, 3, False, False)
 
     rest = pl.ds(CAP, shard - CAP)
     settle(ret.at[0, rest], e_recv.at[0])
 
     def combine_out(at):
-        mixed[:, at] = (nn(weights_hi[...], ret[0, :, at]) + nn(weights_lo[...], ret[0, :, at])).astype(BF16)
+        tokens[:, at] = (nn(weights_hi[...], ret[0, :, at]) + nn(weights_lo[...], ret[0, :, at])).astype(BF16)
 
     chunks(combine_out)
+    stores[0].start()
     settle(ret.at[1, rest], e_recv.at[1])
 
     def combine_back(at):
-        grad_in[:, at] = nn(chosen[...], ret[1, :, at]).astype(BF16)
+        cotangent[:, at] = nn(chosen[...], ret[1, :, at]).astype(BF16)
 
     chunks(combine_back)
-
+    stores[1].start()
+
+    forward(1, 1)
+    backward_pass(1, RIGHT, 2)
+    gradients(1, RIGHT, 2, False, False)
     far(1, 1)
     backward_pass(1, OPPOSITE, 1)
     gradients(1, OPPOSITE, 1, False, True)
+    for copy in stores[2:]:
+        copy.start()
 
     for t in range(2):
         for k in range(2):
@@ -289,6 +318,8 @@
         for i in range(6):
             settle(via.at[t, 0], r_send.at[t, i])
         settle(ret_send.at[t, rest], e_send.at[t])
+    for copy in stores:
+        copy.wait()
 
 
 def solution(mesh):
@@ -314,9 +345,11 @@
                 jax.ShapeDtypeStruct((width, hidden), BF16),
                 jax.ShapeDtypeStruct((hidden, width), BF16),
             ),
-            in_specs=[vmem] * 4 + [hbm] * 3,
-            out_specs=(vmem,) * 5,
+            in_specs=[hbm, vmem, vmem, hbm, hbm, hbm, hbm],
+            out_specs=(hbm,) * 5,
             scratch_shapes=[
+                pltpu.VMEM((n_tok, width), BF16),
+                pltpu.VMEM((n_tok, width), BF16),
                 pltpu.VMEM((width, hidden), BF16),
                 pltpu.VMEM((width, hidden), BF16),
                 pltpu.VMEM((hidden, width), BF16),
@@ -336,7 +369,8 @@
                 pltpu.VMEM((width, hidden), F32),
                 pltpu.VMEM((width, hidden), F32),
                 pltpu.VMEM((hidden, width), F32),
-                dma((3,)),
+                dma((5,)),
+                dma((5,)),
                 dma((2, 2)),
                 dma((2, 2, 2)),
                 dma((2, 2, 6)),
@@ -347,10 +381,10 @@
                 dma((2,)),
             ],
             compiler_params=pltpu.CompilerParams(
-                collective_id=0, has_side_effects=True, vmem_limit_bytes=60 * 2**20
+                collective_id=0, has_side_effects=True, vmem_limit_bytes=48 * 2**20
             ),
             cost_estimate=pl.CostEstimate(flops=flops, bytes_accessed=2 * 8 * n_tok * width, transcendentals=0),
-        )(tokens[0], routes[0], route_weights[0], cotangent[0], w_gate[0], w_up[0], w_down[0])
+        )(tokens[0], routes[0].T, route_weights[0].T, cotangent[0], w_gate[0], w_up[0], w_down[0])
         return tuple(out[None] for out in outs)
 
     return jax.shard_map(

time: 175 us -> 152 us (0.87); the launches traced: 171 us -> 152 us
  Pallas kernels: 159 us -> 144 us
  local copies, waits for them, and re-layouts: 12 us -> 7.4 us
    pallas_call x1, Pallas kernels: 159 us -> 144 us  [per_device(): pl.pallas_call(functools.partial(kernel, n_section, window, step), out_sh...]
    unnamed x15 -> x9, local copies, waits for them, and re-layouts: 12 us -> 7.4 us
where the time goes in v2:
time: 152 us
  Pallas kernels  144 us (95%)
  local copies, waits for them, and re-layouts  7.4 us (5%)
    pallas_call x1, Pallas kernels, per_device(): pl.pallas_call(functools.partial(kernel, n_section, window, step), out_sh...  144 us
    unnamed x9, local copies, waits for them, and re-layouts  7.4 us

profile of v2, /device:TPU:4, one launch (start us, length us, event | category | flops | bytes accessed | tf_op | source)
XLA Modules:
  0.0 151.7 jit_solution(17662143804267004240)
XLA Ops:
  0.6 0.7 copy.17
  1.3 0.7 copy.16
  2.0 143.7 %shard_map.110 = (bf16[256,2560]{1,0:T(8,128)(2,1)S(1)}, bf16[256,2560]{1,0:T(8,128)(2,1)S(1)}, bf16[2560,256]{1,0:T(8,128)(2,1)S(1)}, bf16[2560,256]{1,0:T(8,128)(2,1)S(1)}, bf16[256,2560]{1,0:T(8,128)(2,1)}) custom-call(bf16[256,2560]{1,0:T(8,128)(2,1)} %bitcast.27, s32[6,256]{1,0:T(8,128)S(1)} %bitcast.24, f32[6,256]{1,0:T(8,128)S(1)} %bitcast.25, ...), custom_call_target="tpu_custom_call" | custom-call | flops 10066329600 | bytes 10485760 | tf_op jit(solution)/shard_map/pallas_call | solution.py:339
  145.7 1.1 copy.23
  146.8 1.1 copy.24
  147.8 1.1 copy.25
  148.9 0.0 copy-start
  148.9 1.1 copy.26
  149.9 0.7 copy-done
  150.7 1.1 copy.27
Async XLA Ops:
  148.9 1.8 %copy-start = (bf16[256,2560]{1,0:T(8,128)(2,1)S(1)}, bf16[256,2560]{1,0:T(8,128)(2,1)}, u32[]{:S(2)}) copy-start(bf16[256,2560]{1,0:T(8,128)(2,1)} %get-tuple-element.14) | copy-start | bytes 3932164

commit v3 on v2

--- a/solution.py
+++ b/solution.py
@@ -319,6 +319,15 @@
             settle(via.at[t, 0], r_send.at[t, i])
         settle(ret_send.at[t, rest], e_send.at[t])
     for copy in stores:
+        copy.wait()
+
+
+def hand_over(*refs):
+    n = len(refs) // 2
+    copies = [pltpu.make_async_copy(refs[i], refs[n + i], refs[-1].at[i]) for i in range(n)]
+    for copy in copies:
+        copy.start()
+    for copy in copies:
         copy.wait()
 
 
@@ -381,10 +390,18 @@
                 dma((2,)),
             ],
             compiler_params=pltpu.CompilerParams(
-                collective_id=0, has_side_effects=True, vmem_limit_bytes=48 * 2**20
+                collective_id=0, has_side_effects=True, vmem_limit_bytes=93 * 2**19
             ),
             cost_estimate=pl.CostEstimate(flops=flops, bytes_accessed=2 * 8 * n_tok * width, transcendentals=0),
         )(tokens[0], routes[0].T, route_weights[0].T, cotangent[0], w_gate[0], w_up[0], w_down[0])
+        outs = pl.pallas_call(
+            hand_over,
+            out_shape=tuple(jax.ShapeDtypeStruct(out.shape, out.dtype) for out in outs),
+            in_specs=[hbm] * 5,
+            out_specs=(hbm,) * 5,
+            scratch_shapes=[dma((5,))],
+            compiler_params=pltpu.CompilerParams(vmem_limit_bytes=2**20),
+        )(*outs)
         return tuple(out[None] for out in outs)
 
     return jax.shard_map(

time: 152 us -> 148 us (0.974)
  local copies, waits for them, and re-layouts: 7.4 us -> 1.39 us
  Pallas kernels: 144 us -> 146 us
    unnamed x9 -> x2, local copies, waits for them, and re-layouts: 7.4 us -> 1.39 us
    pallas_call x0 -> x1, Pallas kernels: none -> 2.83 us  [per_device(): pl.pallas_call(hand_over, out_shape=tuple((jax.ShapeDtypeStruct(out.shape...]
where the time goes in v3:
time: 148 us
  Pallas kernels  146 us (99%)
    pallas_call x1, Pallas kernels, per_device(): pl.pallas_call(functools.partial(kernel, n_section, window, step), out_sh...  143 us

profile of v3, /device:TPU:4, one launch (start us, length us, event | category | flops | bytes accessed | tf_op | source)
XLA Modules:
  0.0 147.6 jit_solution(10703580110047095500)
XLA Ops:
  0.6 0.7 copy.17
  1.3 0.7 copy.16
  2.0 142.8 %shard_map.110 = (bf16[256,2560]{1,0:T(8,128)(2,1)S(1)}, bf16[256,2560]{1,0:T(8,128)(2,1)S(1)}, bf16[2560,256]{1,0:T(8,128)(2,1)S(1)}, bf16[2560,256]{1,0:T(8,128)(2,1)S(1)}, bf16[256,2560]{1,0:T(8,128)(2,1)S(1)}) custom-call(bf16[256,2560]{1,0:T(8,128)(2,1)} %bitcast.22, s32[6,256]{1,0:T(8,128)S(1)} %bitcast.20, f32[6,256]{1,0:T(8,128)S(1)} %bitcast.21, ...), custom_call_target="tpu_custom_call" | custom-call | flops 10066329600 | bytes 10485760 | tf_op jit(solution)/shard_map/pallas_call | solution.py:348
  144.8 2.8 %shard_map.111 = (bf16[256,2560]{1,0:T(8,128)(2,1)}, bf16[256,2560]{1,0:T(8,128)(2,1)}, bf16[2560,256]{1,0:T(8,128)(2,1)}, bf16[2560,256]{1,0:T(8,128)(2,1)}, bf16[256,2560]{1,0:T(8,128)(2,1)}) custom-call(bf16[256,2560]{1,0:T(8,128)(2,1)S(1)} %get-tuple-element.15.refs_0_, bf16[256,2560]{1,0:T(8,128)(2,1)S(1)} %get-tuple-element.16.refs_1_, ...), custom_call_target="tpu_custom_call" | custom-call | tf_op jit(solution)/shard_map/pallas_call | solution.py:397

commit v4 on v3

--- a/solution.py
+++ b/solution.py
@@ -14,7 +14,7 @@
 BF16 = jnp.bfloat16
 
 OWN, RIGHT, LEFT, OPPOSITE = range(4)
-ACROSS = ((0, 0), (0, 1))
+ACROSS = (4, 1)
 
 
 def nt(left, right):
@@ -139,25 +139,31 @@
             settle(held.at[t, k, pl.ds(h * half + skip, half - skip)], a_recv.at[t, k, h])
             both_ways(t, k, h, skip, half - skip)
 
+    def hand_on(t, k, h, which, device):
+        count = half - k * ACROSS[t] * CAP
+        if count > 0:
+            rows = [held.at[t, k, pl.ds(w * shard + h * half, count)] for w in (which, OPPOSITE)]
+            remote(*rows, y_send.at[t, k, 4 + h], y_recv.at[t, k, 4 + h], device)
+
     def forward(t, k):
         from_left = [(held.at[t, k, rows_of(LEFT, h)], y_recv.at[t, k, h]) for h in range(2)]
         from_right = [(held.at[t, k, rows_of(RIGHT, h)], y_recv.at[t, k, 2 + h]) for h in range(2)]
         settle(*from_right[0])
-        if k == 0 or (t, 0) not in ACROSS:
-            remote(from_right[0][0], held.at[t, k, rows_of(OPPOSITE, 0)], y_send.at[t, k, 4], y_recv.at[t, k, 4], left)
+        hand_on(t, k, 0, RIGHT, left)
         settle(*from_left[0])
         settle(*from_left[1])
-        if k == 0 or (t, 1) not in ACROSS:
-            remote(from_left[1][0], held.at[t, k, rows_of(OPPOSITE, 1)], y_send.at[t, k, 5], y_recv.at[t, k, 5], right)
+        hand_on(t, k, 1, LEFT, right)
         settle(*from_right[1])
 
     def far(t, k):
         for h in range(2):
             shard_half = held.at[t, k, rows_of(OPPOSITE, h)]
             settle(shard_half, y_recv.at[t, k, 4 + h])
-            if k == 0 and (t, h) in ACROSS:
+            if k == 0 and ACROSS[t] > 0:
+                count = ACROSS[t] * CAP
+                rows = pl.ds(OPPOSITE * shard + (h + 1) * half - count, count)
                 remote(
-                    shard_half, held.at[t, 1, rows_of(OPPOSITE, h)],
+                    held.at[t, 0, rows], held.at[t, 1, rows],
                     y_send.at[t, 1, 4 + h], y_recv.at[t, 1, 4 + h], at_expert(mirror, 0),
                 )
 

time: 148 us -> 146 us (0.986)
  Pallas kernels: 146 us -> 144 us
    pallas_call x1, Pallas kernels: 143 us -> 141 us  [per_device(): pl.pallas_call(functools.partial(kernel, n_section, window, step), out_sh...]
where the time goes in v4:
time: 146 us
  Pallas kernels  144 us (99%)
    pallas_call x1, Pallas kernels, per_device(): pl.pallas_call(functools.partial(kernel, n_section, window, step), out_sh...  141 us

profile of v4, /device:TPU:4, one launch (start us, length us, event | category | flops | bytes accessed | tf_op | source)
XLA Modules:
  0.0 145.9 jit_solution(15896347827953460948)
XLA Ops:
  0.6 0.7 copy.17
  1.3 0.7 copy.16
  2.0 141.0 %shard_map.110 = (bf16[256,2560]{1,0:T(8,128)(2,1)S(1)}, bf16[256,2560]{1,0:T(8,128)(2,1)S(1)}, bf16[2560,256]{1,0:T(8,128)(2,1)S(1)}, bf16[2560,256]{1,0:T(8,128)(2,1)S(1)}, bf16[256,2560]{1,0:T(8,128)(2,1)S(1)}) custom-call(bf16[256,2560]{1,0:T(8,128)(2,1)} %bitcast.22, s32[6,256]{1,0:T(8,128)S(1)} %bitcast.20, f32[6,256]{1,0:T(8,128)S(1)} %bitcast.21, ...), custom_call_target="tpu_custom_call" | custom-call | flops 10066329600 | bytes 10485760 | tf_op jit(solution)/shard_map/pallas_call | solution.py:354
  143.0 2.8 %shard_map.111 = (bf16[256,2560]{1,0:T(8,128)(2,1)}, bf16[256,2560]{1,0:T(8,128)(2,1)}, bf16[2560,256]{1,0:T(8,128)(2,1)}, bf16[2560,256]{1,0:T(8,128)(2,1)}, bf16[256,2560]{1,0:T(8,128)(2,1)}) custom-call(bf16[256,2560]{1,0:T(8,128)(2,1)S(1)} %get-tuple-element.15.refs_0_, bf16[256,2560]{1,0:T(8,128)(2,1)S(1)} %get-tuple-element.16.refs_1_, ...), custom_call_target="tpu_custom_call" | custom-call | tf_op jit(solution)/shard_map/pallas_call | solution.py:403
